TPU v7x, 32 devices: a whole 2x2x4 slice. The times are simulated.
32 devices in a mesh: tile: 8 (over z, x), member: 4 (over y, core).
Axes of the slice: x: 2, y: 2, z: 4, core: 2. Of those that a mesh axis runs over, the one named last changes fastest.
Arguments:
- log_perm: float32 [128, 4, 64, 256], P('member', None, 'tile'), may hold values from -3.4 to 3.4
- start_pressure: float32 [4, 64, 256], P(None, 'tile'), may hold values from -5 to 5
- start_sat: float32 [4, 64, 256], P(None, 'tile'), may hold values from 0.1 to 0.9
- source: float32 [4, 64, 256], P(None, 'tile'), may hold values from -5 to 5
- storage: float32 [4, 64, 256], P(None, 'tile'), may hold values from 0.05 to 0.5
- well_press: float32 [256], replicated, may hold values from -4 to 4
- perf_cell: int32 [2048], P('tile'), may hold values from 0 to 8191
- perf_well: int32 [2048], P('tile'), may hold values from 0 to 255
- perf_count: int32 [8], P('tile'), may hold values from 64 to 256, as said below
- observed: float32 [256], replicated, may hold values from -8 to 8
- obs_var: float32 [256], replicated, may hold values from 0.5 to 5
- obs_noise: float32 [128, 256], P('member'), may hold values from -5 to 5
Outputs:
- new_log_perm: float32 [128, 4, 64, 256], P('member', None, 'tile')
- pressure: float32 [128, 4, 64, 256], P('member', None, 'tile')
- saturation: float32 [128, 4, 64, 256], P('member', None, 'tile')
- well_rates: float32 [128, 256], P('member', 'tile')
Inputs may be any that keep to these rules, and one draw needn't show every extreme that they name: `perf_count`: one strip has all 256 slots live.
All inputs are finite; a program needn't handle non-finite values.
Results may differ from a plain program's by a relative error of at most 0.017.
Values may be sent and summed in bfloat16 or wider, within the bound.
No kernel may reach another device: no remote copies, remote signals or barrier semaphores. Data moves between devices by JAX's collectives and lax.ppermute only.
A program may use at most 64 MiB of HBM per device.

v0:
```python
import jax
import jax.numpy as jnp
from jax import lax
from jax.sharding import PartitionSpec as P

SWEEPS = 2


VERTICAL = 0.5
VISCOSITY_RATIO = 2.0
STEP_COEF = 0.1
INFLATION = 4.0


def extended_2(block, sides, width):
    for axis, dim in sides:
        count = lax.axis_size(axis)
        forward = [(i, i + 1) for i in range(count - 1)]
        backward = [(target, source) for source, target in forward]
        low = lax.ppermute(
            lax.slice_in_dim(block, block.shape[dim] - width, None, axis=dim), axis, forward
        )
        high = lax.ppermute(lax.slice_in_dim(block, 0, width, axis=dim), axis, backward)
        block = jnp.concatenate([low, block, high], axis=dim)
    return block


def harmonic(lower_val, upper_val):
    return 2.0 * lower_val * upper_val / (lower_val + upper_val)


def pad_face(values_in, along_dim, before):
    widths = [(0, 0)] * values_in.ndim
    widths[along_dim] = (1, 0) if before else (0, 1)
    return jnp.pad(values_in, widths)


def slide_by(values_in, along_dim, before):
    extent = values_in.shape[along_dim]
    if before:
        remain = lax.slice_in_dim(values_in, 0, extent - 1, axis=along_dim)
    else:
        remain = lax.slice_in_dim(values_in, 1, extent, axis=along_dim)
    return pad_face(remain, along_dim, before)


def face_terms(permeab, inside):
    face_x = (
        harmonic(permeab[:, :, :-1, :], permeab[:, :, 1:, :]) * (inside[:-1] * inside[1:])[:, None]
    )
    face_y = harmonic(permeab[:, :, :, :-1], permeab[:, :, :, 1:])
    face_z = VERTICAL * harmonic(permeab[:, :-1], permeab[:, 1:])
    return (face_x, face_y, face_z)


def neighbours(face_sets, values_in):
    flow_sum = 0.0
    weight_sum = 0.0
    for faces_dim, along_dim in zip(face_sets, (2, 3, 1)):
        lower = pad_face(faces_dim, along_dim, True)
        upper = pad_face(faces_dim, along_dim, False)
        flow_sum = (
            flow_sum
            + lower * slide_by(values_in, along_dim, True)
            + upper * slide_by(values_in, along_dim, False)
        )
        weight_sum = weight_sum + lower + upper
    return (flow_sum, weight_sum)


def jacobi(pressure, baseline, storage_term, face_sets):
    flow_sum, weight_sum = neighbours(face_sets, pressure)
    return (baseline + flow_sum) / (storage_term + weight_sum)


def water_frac(values_in):
    squared = values_in * values_in
    return squared / (squared + VISCOSITY_RATIO * (1.0 - values_in) * (1.0 - values_in))


def transport(pressure, saturation, face_sets):
    fraction = water_frac(saturation)
    change = 0.0
    for faces_dim, along_dim in zip(face_sets, (2, 3, 1)):
        extent = pressure.shape[along_dim]
        lower_press = lax.slice_in_dim(pressure, 0, extent - 1, axis=along_dim)
        upper_press = lax.slice_in_dim(pressure, 1, extent, axis=along_dim)
        lower_frac = lax.slice_in_dim(fraction, 0, extent - 1, axis=along_dim)
        upper_frac = lax.slice_in_dim(fraction, 1, extent, axis=along_dim)
        velocity = faces_dim * (lower_press - upper_press)
        carried = velocity * jnp.where(velocity > 0, lower_frac, upper_frac)
        change = change + pad_face(carried, along_dim, True) - pad_face(carried, along_dim, False)
    return saturation + STEP_COEF * change


def solve_spd(gram_matrix, cross_matrix):
    factor = jnp.linalg.cholesky(gram_matrix + jnp.eye(gram_matrix.shape[0], dtype=jnp.float32))
    halfway = lax.linalg.triangular_solve(factor, cross_matrix, left_side=True, lower=True)
    return lax.linalg.triangular_solve(
        factor, halfway, left_side=True, lower=True, transpose_a=True
    )


def trim_rim(values_in, rim_cut):
    return values_in[:, :, rim_cut : values_in.shape[2] - rim_cut, :]


def per_device(
    log_perm,
    start_pressure,
    start_sat,
    source,
    storage,
    well_press,
    perf_cell,
    perf_well,
    perf_count,
    observed,
    obs_var,
    obs_noise,
):
    local_count, layers, strip_width, strip_depth = log_perm.shape
    tile_count = lax.axis_size("tile")
    members = local_count * lax.axis_size("member")
    well_count = well_press.shape[0]
    well_share = well_count // tile_count
    tile_rank = lax.axis_index("tile")
    member_rank = lax.axis_index("member")
    permeab = jnp.exp(extended_2(log_perm, (("tile", 2),), 1))
    shared = extended_2(jnp.stack([start_pressure, start_sat]), (("tile", 2),), 1)
    column = tile_rank * strip_width - 1 + jnp.arange(strip_width + 2 * 1, dtype=jnp.int32)
    face_sets = face_terms(
        permeab, ((column >= 0) & (column < strip_width * tile_count)).astype(jnp.float32)
    )
    baseline = jnp.pad(source + storage * start_pressure, ((0, 0), (1, 1), (0, 0)))[None]
    storage_term = jnp.pad(storage, ((0, 0), (1, 1), (0, 0)), constant_values=1.0)[None]
    extended = jnp.broadcast_to(shared[0:1], (local_count,) + shared.shape[1:])
    for sweep_idx in range(SWEEPS):
        pressure = trim_rim(jacobi(extended, baseline, storage_term, face_sets), 1)
        extended = extended_2(pressure, (("tile", 2),), 1)
    saturation = trim_rim(transport(extended, shared[1:2], face_sets), 1)
    permeab = trim_rim(permeab, 1)
    cell_count = layers * strip_width * strip_depth
    mobility = (permeab * water_frac(saturation)).reshape(local_count, cell_count)
    cell_press = pressure.reshape(local_count, cell_count)
    perf_mob = jnp.take(mobility, perf_cell, axis=1)
    perf_press = jnp.take(cell_press, perf_cell, axis=1)
    selector = (perf_well[:, None] == jnp.arange(well_count, dtype=jnp.int32)[None, :]).astype(
        jnp.float32
    )
    perf_bhp = jnp.dot(selector, well_press, precision=lax.Precision.HIGHEST)
    live_mask = (jnp.arange(perf_cell.shape[0], dtype=jnp.int32) < perf_count[0]).astype(
        jnp.float32
    )
    perf_terms = perf_mob * (perf_press - perf_bhp[None]) * live_mask[None]
    partial_rates = jnp.dot(
        perf_terms, selector, precision=lax.Precision.HIGHEST, preferred_element_type=jnp.float32
    )
    member_root = (members - 1) ** 0.5
    spread = jnp.sqrt(INFLATION * obs_var)
    well_rates = lax.psum_scatter(partial_rates, "tile", scatter_dimension=1, tiled=True)
    well_first = tile_rank * well_share
    spread_part = lax.dynamic_slice_in_dim(spread, well_first, well_share, 0)
    observed_part = lax.dynamic_slice_in_dim(observed, well_first, well_share, 0)
    noise_part = lax.dynamic_slice_in_dim(obs_noise, well_first, well_share, 1)
    mean_rate = lax.psum(jnp.sum(well_rates, 0), "member") / members
    scaled = (well_rates - mean_rate) / (spread_part * member_root)
    innovation = (observed_part - well_rates) / spread_part + noise_part
    scaled_all, innov_all = (
        lax.all_gather(scaled, "member", axis=0, tiled=True),
        lax.all_gather(innovation, "member", axis=0, tiled=True),
    )
    gram_part = jnp.dot(
        scaled_all,
        scaled_all.T,
        precision=lax.Precision.HIGHEST,
        preferred_element_type=jnp.float32,
    )
    cross_part = jnp.dot(
        scaled_all, innov_all.T, precision=lax.Precision.HIGHEST, preferred_element_type=jnp.float32
    )
    gram_matrix, cross_matrix = lax.psum((gram_part, cross_part), "tile")
    weights_low = solve_spd(gram_matrix, cross_matrix).astype(jnp.bfloat16)
    anomaly = (log_perm / member_root).astype(jnp.bfloat16).reshape(local_count, cell_count)
    first_member = member_rank * local_count
    contract = (((0,), (0,)), ((), ()))
    own_rows = lax.dynamic_slice_in_dim(weights_low, first_member, local_count, 0)
    update_sum = lax.psum_scatter(
        lax.dot_general(own_rows, anomaly, contract, preferred_element_type=jnp.float32).astype(
            jnp.bfloat16
        ),
        "member",
        scatter_dimension=0,
        tiled=True,
    ).astype(jnp.float32)
    new_log_perm = log_perm + update_sum.reshape(log_perm.shape)
    return (new_log_perm, pressure, saturation, well_rates)


def solution(mesh):
    return jax.shard_map(
        per_device,
        mesh=mesh,
        in_specs=(
            P("member", None, "tile", None),
            P(None, "tile", None),
            P(None, "tile", None),
            P(None, "tile", None),
            P(None, "tile", None),
            P(),
            P("tile"),
            P("tile"),
            P("tile"),
            P(),
            P(),
            P("member", None),
        ),
        out_specs=(
            P("member", None, "tile", None),
            P("member", None, "tile", None),
            P("member", None, "tile", None),
            P("member", "tile"),
        ),
        check_vma=False,
    )
```

profile of v0, /device:TPU:0, one launch (start us, length us, event | category | flops | bytes accessed | tf_op | source)
XLA Modules:
  0.0 286.3 jit_solution(4038910882344599983)
XLA Ops:
  7.3 1.9 copy.19
  9.2 4.8 %collective-permute-start = (f32[32,4,1,256]{3,0,2,1:T(8,128)S(1)}, f32[32,4,1,256]{3,0,2,1:T(8,128)S(1)}, u32[]{:S(2)}, u32[]{:S(2)}) collective-permute-start(f32[32,4,1,256]{3,0,2,1:T(8,128)S(1)} %get-tuple-element.23), channel_id=1, source_target_pairs={{0,4},{4,8},{8,12},{12,16},{16,20},{20,24},{24,28},{1,5},{5,9},{9,... | collective-permute-start | bytes 393224 | tf_op jit(solution)/shard_map/ppermute | solution.py:20
  14.1 1.3 collective-permute-start.1
  15.4 4.5 %collective-permute-start.2 = (f32[2,4,1,256]{3,2,1,0:T(1,128)S(1)}, f32[2,4,1,256]{3,2,1,0:T(1,128)S(1)}, u32[]{:S(2)}, u32[]{:S(2)}) collective-permute-start(f32[2,4,1,256]{3,2,1,0:T(1,128)S(1)} %get-tuple-element.40), channel_id=1, source_target_pairs={{0,4},{4,8},{8,12},{12,16},{16,20},{20,24},{24,28},{1,5},{5,9},{9,... | collective-permute-start | bytes 24584 | tf_op jit(solution)/shard_map/ppermute | solution.py:20
  20.0 1.3 collective-permute-start.3
  22.0 0.5 compare_and_fusion
  22.6 0.9 fusion.25
  23.5 0.6 dynamic_slice.13
  24.1 1.8 collective-permute-done.3
  26.1 0.6 slice.253
  26.8 0.2 maximum_exponential_fusion
  27.0 0.4 add_divide_fusion.1
  27.4 0.2 divide_multiply_fusion.1
  27.6 0.3 divide_multiply_fusion
  27.9 0.1 broadcast_in_dim.101
  28.0 0.1 broadcast_in_dim.102
  28.4 2.1 fusion.3
  30.6 4.8 %collective-permute-start.4 = (f32[32,4,1,256]{3,0,2,1:T(8,128)S(1)}, f32[32,4,1,256]{3,0,2,1:T(8,128)S(1)}, u32[]{:S(2)}, u32[]{:S(2)}) collective-permute-start(f32[32,4,1,256]{3,0,2,1:T(8,128)S(1)} %get-tuple-element.21), channel_id=1, source_target_pairs={{0,4},{4,8},{8,12},{12,16},{16,20},{20,24},{24,28},{1,5},{5,9},{9,... | collective-permute-start | bytes 393224 | tf_op jit(solution)/shard_map/ppermute | solution.py:20
  35.4 1.3 collective-permute-start.5
  36.8 0.1 slice.232
  36.9 1.0 collective-permute-done.4
  37.9 4.4 %collective-permute-done.5 = f32[32,4,1,256]{3,0,2,1:T(8,128)S(1)} collective-permute-done((f32[32,4,1,256]{3,0,2,1:T(8,128)S(1)}, f32[32,4,1,256]{3,0,2,1:T(8,128)S(1)}, u32[]{:S(2)}, u32[]{:S(2)}) %collective-permute-start.5) | collective-permute-done | bytes 131104 | tf_op jit(solution)/shard_map/ppermute | solution.py:23
  42.3 0.1 pad_maximum_fusion
  42.4 0.5 fusion.48
  42.9 0.2 fusion.49
  43.2 2.1 fusion.7
  45.3 4.1 %collective-permute-start.6 = (f32[32,4,1,256]{3,0,2,1:T(8,128)S(1)}, f32[32,4,1,256]{3,0,2,1:T(8,128)S(1)}, u32[]{:S(2)}, u32[]{:S(2)}) collective-permute-start(f32[32,4,1,256]{3,0,2,1:T(8,128)S(1)} %get-tuple-element.15), channel_id=1, source_target_pairs={{0,4},{4,8},{8,12},{12,16},{16,20},{20,24},{24,28},{1,5},{5,9},{9,... | collective-permute-start | bytes 393224 | tf_op jit(solution)/shard_map/ppermute | solution.py:20
  49.4 1.3 collective-permute-start.7
  50.8 2.7 copy.23
  53.5 2.9 %gather_fusion.1 = f32[256,32]{1,0:T(8,128)S(1)} fusion(f32[32,8192]{0,1:T(8,128)} %bitcast.72, s32[1024]{0:T(1024)S(1)} %pad_clamp_fusion), kind=kCustom, calls=%fused_computation.1.clone | custom fusion | bytes 66560 | tf_op jit(solution)/shard_map/jit(_take)/gather | solution.py:147
  56.5 0.8 select_multiply_fusion
  57.3 0.4 select_multiply_fusion.2
  57.7 0.5 select_multiply_fusion.1
  58.2 0.2 copy-done.4
  58.5 1.7 fusion.23
  60.1 2.7 copy.22
  62.8 3.0 %gather_fusion = f32[256,32]{1,0:T(8,128)S(1)} fusion(f32[32,8192]{0,1:T(8,128)} %bitcast.71, s32[1024]{0:T(1024)S(1)} %pad_clamp_fusion), kind=kCustom, calls=%fused_computation.clone | custom fusion | bytes 66560 | tf_op jit(solution)/shard_map/jit(_take)/gather | solution.py:146
  65.8 1.2 convolution_bitcast_fusion
  67.2 62.3 %reduce-scatter.7.cloned.1.call-done = f32[32,32]{1,0:T(8,128)} async-done(((f32[256,32]{1,0:T(8,128)}), f32[32,32]{1,0:T(8,128)}) %reduce-scatter.7.cloned.1.call-update) | async-done | bytes 4112
  129.5 0.8 copy.28
  130.3 0.8 bitcast_reduce_fusion
  131.1 5.7 %psum.21 = f32[32]{0:T(128)S(1)} all-reduce(f32[32]{0:T(128)S(1)} %bitcast_reduce_fusion), channel_id=1, replica_groups=mesh['tile'=8,'member'=4] {'member'}, use_global_device_ids=true, to_apply=%region_2.4 | all-reduce | flops 32 | bytes 256 | tf_op jit(solution)/shard_map/psum | solution.py:166
  136.9 5.2 %all_gather.6 = f32[128,32]{1,0:T(8,128)S(1)} all-gather(f32[32,32]{1,0:T(8,128)S(1)} %get-tuple-element.43), channel_id=1, replica_groups=mesh['tile'=8,'member'=4] {'member'}, dimensions={0}, use_global_device_ids=true | all-gather | bytes 20480 | tf_op jit(solution)/shard_map/all_gather | solution.py:170
  142.1 5.2 %all_gather.7 = f32[128,32]{1,0:T(8,128)S(1)} all-gather(f32[32,32]{1,0:T(8,128)S(1)} %get-tuple-element.42), channel_id=1, replica_groups=mesh['tile'=8,'member'=4] {'member'}, dimensions={0}, use_global_device_ids=true | all-gather | bytes 20480 | tf_op jit(solution)/shard_map/all_gather | solution.py:171
  147.3 0.9 fusion.54
  148.2 0.9 fusion.55
  149.2 0.2 reduce-scatter.5.cloned.1.call-start
  149.4 0.1 multiply_convert_fusion
  149.5 0.3 copy.30
  149.9 68.6 %all-reduce.29.cloned.1.call-done = (f32[128,128]{1,0:T(8,128)}, f32[128,128]{1,0:T(8,128)}) async-done(((f32[128,128]{1,0:T(8,128)}, f32[128,128]{1,0:T(8,128)}), (f32[128,128]{1,0:T(8,128)}, f32[128,128]{1,0:T(8,128)})) %all-reduce.29.cloned.1.call-update) | async-done | bytes 131088 | tf_op jit(solution)/shard_map/psum | solution.py:182
  218.5 0.9 convert_add_fusion
  219.4 0.9 fusion.39
  220.3 11.7 %cholesky.17 = f32[128,128]{1,0:T(8,128)S(1)} custom-call(f32[128,128]{1,0:T(8,128)S(1)} %fusion.39), custom_call_target="Cholesky" | custom-call | tf_op jit(solution)/shard_map/jit(cholesky)/cholesky | solution.py:97
  232.0 0.6 compare_reduce_fusion
  232.7 0.7 fusion.34
  233.4 9.8 %custom-call.8 = f32[1,128,128]{1,2,0:T(8,128)S(1)} custom-call(f32[1,128,128]{2,1,0:T(8,128)S(1)} %fusion.34), custom_call_target="InvertDiagBlocksLowerTriangular" | custom-call | tf_op jit(solution)/shard_map/triangular_solve | solution.py:99
  243.2 1.1 fusion.37
  244.3 0.2 fusion.35
  244.5 2.1 convolution_convert_fusion
  246.6 1.6 copy.25
  248.2 1.6 copy.26
  249.8 27.7 %reduce-scatter.5.cloned.1.call-done = bf16[32,8192]{1,0:T(8,128)(2,1)} async-done(((bf16[128,8192]{1,0:T(8,128)(2,1)}), bf16[32,8192]{1,0:T(8,128)(2,1)}) %reduce-scatter.5.cloned.1.call-update) | async-done | bytes 524304 | tf_op jit(solution)/shard_map/reduce_scatter | solution.py:188
  277.5 1.2 copy.31
  278.6 1.1 add.253
  (76 shorter events, 1.4 us)
Async XLA Ops:
  7.2 15.4 %copy-start = (f32[256]{0:T(256)S(1)}, f32[256]{0:T(256)}, u32[]{:S(2)}) copy-start(f32[256]{0:T(256)} %param.19) | copy-start | bytes 3076
  7.2 8.2 %copy-start.3 = (f32[4,8,256]{2,1,0:T(8,128)S(1)}, f32[4,8,256]{2,1,0:T(8,128)}, u32[]{:S(2)}) copy-start(f32[4,8,256]{2,1,0:T(8,128)} %param.15) | copy-start | bytes 98308
  7.2 8.2 %copy-start.6 = (f32[4,8,256]{2,1,0:T(8,128)S(1)}, f32[4,8,256]{2,1,0:T(8,128)}, u32[]{:S(2)}) copy-start(f32[4,8,256]{2,1,0:T(8,128)} %param.16) | copy-start | bytes 98308
  7.2 14.2 %copy-start.10 = (s32[256]{0:T(256)S(1)}, s32[256]{0:T(256)}, u32[]{:S(2)}) copy-start(s32[256]{0:T(256)} %param.20) | copy-start | bytes 3076
  7.2 15.3 %copy-start.15 = (f32[256]{0:T(256)S(1)}, f32[256]{0:T(256)}, u32[]{:S(2)}) copy-start(f32[256]{0:T(256)} %param.24) | copy-start | bytes 3076
  7.2 15.3 %copy-start.8 = (f32[4,8,256]{2,1,0:T(8,128)S(1)}, f32[4,8,256]{2,1,0:T(8,128)}, u32[]{:S(2)}) copy-start(f32[4,8,256]{2,1,0:T(8,128)} %param.17) | copy-start | bytes 98308
  7.2 15.3 %copy-start.5 = (f32[4,8,256]{2,1,0:T(8,128)S(1)}, f32[4,8,256]{2,1,0:T(8,128)}, u32[]{:S(2)}) copy-start(f32[4,8,256]{2,1,0:T(8,128)} %param.18) | copy-start | bytes 98308
  7.2 15.3 %copy-start.12 = (s32[256]{0:T(256)S(1)}, s32[256]{0:T(256)}, u32[]{:S(2)}) copy-start(s32[256]{0:T(256)} %param.21) | copy-start | bytes 3076
  7.3 16.3 %copy-start.17 = (f32[256]{0:T(256)S(1)}, f32[256]{0:T(256)}, u32[]{:S(2)}) copy-start(f32[256]{0:T(256)} %param.23) | copy-start | bytes 3076
  7.3 122.2 %reduce-scatter.7.cloned.1.call-start = ((), (), s32[]{:S(2)}) async-start(), calls=%async_computation.3 | async-start | bytes 147456
  9.2 17.5 %collective-permute-start = (f32[32,4,1,256]{3,0,2,1:T(8,128)S(1)}, f32[32,4,1,256]{3,0,2,1:T(8,128)S(1)}, u32[]{:S(2)}, u32[]{:S(2)}) collective-permute-start(f32[32,4,1,256]{3,0,2,1:T(8,128)S(1)} %get-tuple-element.23), channel_id=1, source_target_pairs={{0,4},{4,8},{8,12},{12,16},{16,20},{20,24},{24,28},{1,5},{5,9},{9,... | collective-permute-start | bytes 393224 | tf_op jit(solution)/shard_map/ppermute | solution.py:20
  14.1 12.7 %collective-permute-start.1 = (f32[32,4,1,256]{3,0,2,1:T(8,128)S(1)}, f32[32,4,1,256]{3,0,2,1:T(8,128)S(1)}, u32[]{:S(2)}, u32[]{:S(2)}) collective-permute-start(f32[32,4,1,256]{3,0,2,1:T(8,128)S(1)} %get-tuple-element.24), channel_id=1, source_target_pairs={{4,0},{8,4},{12,8},{16,12},{20,16},{24,20},{28,24},{5,1},{9,5},{13... | collective-permute-start | bytes 393224 | tf_op jit(solution)/shard_map/ppermute | solution.py:23
  15.4 8.7 %collective-permute-start.2 = (f32[2,4,1,256]{3,2,1,0:T(1,128)S(1)}, f32[2,4,1,256]{3,2,1,0:T(1,128)S(1)}, u32[]{:S(2)}, u32[]{:S(2)}) collective-permute-start(f32[2,4,1,256]{3,2,1,0:T(1,128)S(1)} %get-tuple-element.40), channel_id=1, source_target_pairs={{0,4},{4,8},{8,12},{12,16},{16,20},{20,24},{24,28},{1,5},{5,9},{9,... | collective-permute-start | bytes 24584 | tf_op jit(solution)/shard_map/ppermute | solution.py:20
  20.0 6.0 %collective-permute-start.3 = (f32[2,4,1,256]{3,2,1,0:T(1,128)S(1)}, f32[2,4,1,256]{3,2,1,0:T(1,128)S(1)}, u32[]{:S(2)}, u32[]{:S(2)}) collective-permute-start(f32[2,4,1,256]{3,2,1,0:T(1,128)S(1)} %get-tuple-element.41), channel_id=1, source_target_pairs={{4,0},{8,4},{12,8},{16,12},{20,16},{24,20},{28,24},{5,1},{9,5},{13... | collective-permute-start | bytes 24584 | tf_op jit(solution)/shard_map/ppermute | solution.py:23
  30.6 7.3 %collective-permute-start.4 = (f32[32,4,1,256]{3,0,2,1:T(8,128)S(1)}, f32[32,4,1,256]{3,0,2,1:T(8,128)S(1)}, u32[]{:S(2)}, u32[]{:S(2)}) collective-permute-start(f32[32,4,1,256]{3,0,2,1:T(8,128)S(1)} %get-tuple-element.21), channel_id=1, source_target_pairs={{0,4},{4,8},{8,12},{12,16},{16,20},{20,24},{24,28},{1,5},{5,9},{9,... | collective-permute-start | bytes 393224 | tf_op jit(solution)/shard_map/ppermute | solution.py:20
  35.4 6.9 %collective-permute-start.5 = (f32[32,4,1,256]{3,0,2,1:T(8,128)S(1)}, f32[32,4,1,256]{3,0,2,1:T(8,128)S(1)}, u32[]{:S(2)}, u32[]{:S(2)}) collective-permute-start(f32[32,4,1,256]{3,0,2,1:T(8,128)S(1)} %get-tuple-element.22), channel_id=1, source_target_pairs={{4,0},{8,4},{12,8},{16,12},{20,16},{24,20},{28,24},{5,1},{9,5},{13... | collective-permute-start | bytes 393224 | tf_op jit(solution)/shard_map/ppermute | solution.py:23
  45.3 11.0 %collective-permute-start.6 = (f32[32,4,1,256]{3,0,2,1:T(8,128)S(1)}, f32[32,4,1,256]{3,0,2,1:T(8,128)S(1)}, u32[]{:S(2)}, u32[]{:S(2)}) collective-permute-start(f32[32,4,1,256]{3,0,2,1:T(8,128)S(1)} %get-tuple-element.15), channel_id=1, source_target_pairs={{0,4},{4,8},{8,12},{12,16},{16,20},{20,24},{24,28},{1,5},{5,9},{9,... | collective-permute-start | bytes 393224 | tf_op jit(solution)/shard_map/ppermute | solution.py:20
  49.4 7.0 %collective-permute-start.7 = (f32[32,4,1,256]{3,0,2,1:T(8,128)S(1)}, f32[32,4,1,256]{3,0,2,1:T(8,128)S(1)}, u32[]{:S(2)}, u32[]{:S(2)}) collective-permute-start(f32[32,4,1,256]{3,0,2,1:T(8,128)S(1)} %get-tuple-element.16), channel_id=1, source_target_pairs={{4,0},{8,4},{12,8},{16,12},{20,16},{24,20},{28,24},{5,1},{9,5},{13... | collective-permute-start | bytes 393224 | tf_op jit(solution)/shard_map/ppermute | solution.py:23
  57.7 0.8 copy-start.4
  60.1 5.7 %copy-start.11 = (pred[256]{0:T(512)(128)(4,1)S(1)}, pred[256]{0:T(512)(128)(4,1)}, u32[]{:S(2)}) copy-start(pred[256]{0:T(512)(128)(4,1)} %get-tuple-element.44) | copy-start | bytes 772
  60.1 5.7 %copy-start.13 = (s32[256]{0:T(256)S(1)}, s32[256]{0:T(256)}, u32[]{:S(2)}) copy-start(s32[256]{0:T(256)} %param.21) | copy-start | bytes 3076
  60.1 5.7 %copy-start.14 = (f32[1,256]{1,0:T(1,128)S(1)}, f32[1,256]{1,0:T(1,128)}, u32[]{:S(2)}) copy-start(f32[1,256]{1,0:T(1,128)} %fusion.25) | copy-start | bytes 3076
  60.1 76.6 %copy-start.9 = (f32[32,256]{1,0:T(8,128)S(1)}, f32[32,256]{1,0:T(8,128)}, u32[]{:S(2)}) copy-start(f32[32,256]{1,0:T(8,128)} %param.25) | copy-start | bytes 98308
  60.1 76.6 %copy-start.16 = (f32[32]{0:T(128)S(1)}, f32[32]{0:T(128)}, u32[]{:S(2)}) copy-start(f32[32]{0:T(128)} %dynamic_slice.13) | copy-start | bytes 388
  62.8 86.6 %copy-start.1 = (f32[32,4,8,256]{3,2,1,0:T(8,128)S(1)}, f32[32,4,8,256]{3,2,1,0:T(8,128)}, u32[]{:S(2)}) copy-start(f32[32,4,8,256]{3,2,1,0:T(8,128)} %param.14) | copy-start | bytes 3145732
  67.1 151.4 %all-reduce.29.cloned.1.call-start = ((), (), s32[]{:S(2)}) async-start(), calls=%async_computation.4 | async-start | bytes 262144 | tf_op jit(solution)/shard_map/psum | solution.py:182
  130.3 19.6 %copy-start.7 = (f32[32,32]{1,0:T(8,128)}, f32[32,32]{1,0:T(8,128)S(1)}, u32[]{:S(2)}) copy-start(f32[32,32]{1,0:T(8,128)S(1)} %copy.28) | copy-start | bytes 12292
  149.2 128.3 %reduce-scatter.5.cloned.1.call-start = ((), (), s32[]{:S(2)}) async-start(), calls=%async_computation.2 | async-start | bytes 2621440 | tf_op jit(solution)/shard_map/reduce_scatter | solution.py:188
  246.6 1.6 copy-start.2
Sparse Core Ops, SparseCore 0:
  67.2 62.2 reduce-scatter.6
  149.3 69.1 all-reduce.28
  246.8 30.6 reduce-scatter.4
where the time goes:
time: 287 us; the launch traced here: 286 us
  waiting for transfers between devices  166 us (58%)
  other arithmetic  36.4 us (13%)
  starting transfers between devices  23.8 us (8%)
  local copies, waits for them, and re-layouts  21.8 us (8%)
  blocking collectives  16.1 us (6%)
  between operations  15 us (5%)
  matrix products  7.33 us (3%)
    psum x1, waiting for transfers between devices, per_device(): gram_matrix, cross_matrix = lax.psum((gram_part, cross_part), 'tile')  68.6 us
    unnamed x4, waiting for transfers between devices  62.3 us
    reduce_scatter x1, waiting for transfers between devices, per_device(): lax.psum_scatter(lax.dot_general(own_rows, anomaly, contract, preferred_e...  27.7 us
    ppermute x4, starting transfers between devices, extended_2(): lax.ppermute(lax.slice_in_dim(block, block.shape[dim] - width, None, axis...  18.3 us
    another operation x3, other arithmetic, solve_spd(): jnp.linalg.cholesky(gram_matrix + jnp.eye(gram_matrix.shape[0], dtype=jnp...  12.4 us
    another operation x2, other arithmetic, solve_spd(): lax.linalg.triangular_solve(factor, halfway, left_side=True, lower=True,...  10.5 us
    unnamed x42, local copies, waits for them, and re-layouts  7.59 us
    ppermute x4, waiting for transfers between devices, extended_2(): lax.ppermute(lax.slice_in_dim(block, 0, width, axis=dim), axis, backward)  6.19 us
  transfers between devices with their start and end apart: 11, of which 6 were waited for; matrix products, arithmetic and copies ran while one was open for 4% of the time, Pallas kernels for 0%

commit v1 on v0

--- a/solution.py
+++ b/solution.py
@@ -12,17 +12,15 @@
 INFLATION = 4.0
 
 
-def extended_2(block, sides, width):
-    for axis, dim in sides:
-        count = lax.axis_size(axis)
-        forward = [(i, i + 1) for i in range(count - 1)]
-        backward = [(target, source) for source, target in forward]
-        low = lax.ppermute(
-            lax.slice_in_dim(block, block.shape[dim] - width, None, axis=dim), axis, forward
-        )
-        high = lax.ppermute(lax.slice_in_dim(block, 0, width, axis=dim), axis, backward)
-        block = jnp.concatenate([low, block, high], axis=dim)
-    return block
+def halo_rows(block, axis, dim, width):
+    count = lax.axis_size(axis)
+    forward = [(i, i + 1) for i in range(count - 1)]
+    backward = [(target, source) for source, target in forward]
+    low = lax.ppermute(
+        lax.slice_in_dim(block, block.shape[dim] - width, None, axis=dim), axis, forward
+    )
+    high = lax.ppermute(lax.slice_in_dim(block, 0, width, axis=dim), axis, backward)
+    return low.astype(jnp.float32), high.astype(jnp.float32)
 
 
 def harmonic(lower_val, upper_val):
@@ -126,20 +124,27 @@
     well_share = well_count // tile_count
     tile_rank = lax.axis_index("tile")
     member_rank = lax.axis_index("member")
-    permeab = jnp.exp(extended_2(log_perm, (("tile", 2),), 1))
-    shared = extended_2(jnp.stack([start_pressure, start_sat]), (("tile", 2),), 1)
-    column = tile_rank * strip_width - 1 + jnp.arange(strip_width + 2 * 1, dtype=jnp.int32)
-    face_sets = face_terms(
-        permeab, ((column >= 0) & (column < strip_width * tile_count)).astype(jnp.float32)
-    )
-    baseline = jnp.pad(source + storage * start_pressure, ((0, 0), (1, 1), (0, 0)))[None]
-    storage_term = jnp.pad(storage, ((0, 0), (1, 1), (0, 0)), constant_values=1.0)[None]
-    extended = jnp.broadcast_to(shared[0:1], (local_count,) + shared.shape[1:])
+    rim = SWEEPS + 1
+    fields = jnp.stack([start_pressure, start_sat, source, storage])
+    packed = jnp.concatenate([log_perm, fields], axis=0).astype(jnp.bfloat16)
+    low, high = halo_rows(packed, "tile", 2, rim)
+    wide_perm = jnp.concatenate([low[:local_count], log_perm, high[:local_count]], axis=2)
+    wide_fields = jnp.concatenate([low[local_count:], fields, high[local_count:]], axis=2)
+    wide_press, wide_sat, wide_source, wide_storage = (wide_fields[i] for i in range(4))
+    anomaly = (log_perm / (members - 1) ** 0.5).astype(jnp.bfloat16).reshape(local_count, -1)
+    anomaly_all = lax.all_gather(anomaly, "member", axis=0, tiled=True)
+    permeab = jnp.exp(wide_perm)
+    column = tile_rank * strip_width - rim + jnp.arange(strip_width + 2 * rim, dtype=jnp.int32)
+    inside = ((column >= 0) & (column < strip_width * tile_count)).astype(jnp.float32)
+    face_sets = face_terms(permeab, inside)
+    baseline = (wide_source + wide_storage * wide_press)[None]
+    storage_term = jnp.where(inside[:, None] > 0, wide_storage, 1.0)[None]
+    extended = jnp.broadcast_to(wide_press[None], wide_perm.shape)
     for sweep_idx in range(SWEEPS):
-        pressure = trim_rim(jacobi(extended, baseline, storage_term, face_sets), 1)
-        extended = extended_2(pressure, (("tile", 2),), 1)
-    saturation = trim_rim(transport(extended, shared[1:2], face_sets), 1)
-    permeab = trim_rim(permeab, 1)
+        extended = jacobi(extended, baseline, storage_term, face_sets)
+    pressure = trim_rim(extended, rim)
+    saturation = trim_rim(transport(extended, wide_sat[None], face_sets), rim)
+    permeab = trim_rim(permeab, rim)
     cell_count = layers * strip_width * strip_depth
     mobility = (permeab * water_frac(saturation)).reshape(local_count, cell_count)
     cell_press = pressure.reshape(local_count, cell_count)
@@ -158,41 +163,28 @@
     )
     member_root = (members - 1) ** 0.5
     spread = jnp.sqrt(INFLATION * obs_var)
-    well_rates = lax.psum_scatter(partial_rates, "tile", scatter_dimension=1, tiled=True)
-    well_first = tile_rank * well_share
-    spread_part = lax.dynamic_slice_in_dim(spread, well_first, well_share, 0)
-    observed_part = lax.dynamic_slice_in_dim(observed, well_first, well_share, 0)
-    noise_part = lax.dynamic_slice_in_dim(obs_noise, well_first, well_share, 1)
-    mean_rate = lax.psum(jnp.sum(well_rates, 0), "member") / members
-    scaled = (well_rates - mean_rate) / (spread_part * member_root)
-    innovation = (observed_part - well_rates) / spread_part + noise_part
-    scaled_all, innov_all = (
-        lax.all_gather(scaled, "member", axis=0, tiled=True),
-        lax.all_gather(innovation, "member", axis=0, tiled=True),
-    )
-    gram_part = jnp.dot(
-        scaled_all,
-        scaled_all.T,
-        precision=lax.Precision.HIGHEST,
-        preferred_element_type=jnp.float32,
-    )
-    cross_part = jnp.dot(
-        scaled_all, innov_all.T, precision=lax.Precision.HIGHEST, preferred_element_type=jnp.float32
-    )
-    gram_matrix, cross_matrix = lax.psum((gram_part, cross_part), "tile")
+    traded = lax.all_to_all(
+        partial_rates.reshape(local_count, tile_count, well_share).transpose(1, 0, 2), "tile", 0, 0
+    )
+    well_rates = jnp.sum(traded, 0)
+    every = lax.all_gather(well_rates, ("member", "tile"), axis=0)
+    every = every.reshape(members // local_count, tile_count, local_count, well_share)
+    rates_all = every.transpose(0, 2, 1, 3).reshape(members, well_count)
+    mean_rate = jnp.sum(rates_all, 0) / members
+    scaled = (rates_all - mean_rate) / (spread * member_root)
+    gram_matrix = jnp.dot(
+        scaled, scaled.T, precision=lax.Precision.HIGHEST, preferred_element_type=jnp.float32
+    )
+    own_rates = lax.dynamic_slice_in_dim(rates_all, member_rank * local_count, local_count, 0)
+    own_innov = (observed - own_rates) / spread + obs_noise
+    cross_matrix = jnp.dot(
+        scaled, own_innov.T, precision=lax.Precision.HIGHEST, preferred_element_type=jnp.float32
+    )
     weights_low = solve_spd(gram_matrix, cross_matrix).astype(jnp.bfloat16)
-    anomaly = (log_perm / member_root).astype(jnp.bfloat16).reshape(local_count, cell_count)
-    first_member = member_rank * local_count
     contract = (((0,), (0,)), ((), ()))
-    own_rows = lax.dynamic_slice_in_dim(weights_low, first_member, local_count, 0)
-    update_sum = lax.psum_scatter(
-        lax.dot_general(own_rows, anomaly, contract, preferred_element_type=jnp.float32).astype(
-            jnp.bfloat16
-        ),
-        "member",
-        scatter_dimension=0,
-        tiled=True,
-    ).astype(jnp.float32)
+    update_sum = lax.dot_general(
+        weights_low, anomaly_all, contract, preferred_element_type=jnp.float32
+    )
     new_log_perm = log_perm + update_sum.reshape(log_perm.shape)
     return (new_log_perm, pressure, saturation, well_rates)
 

time: 287 us -> 177 us (0.62)
  waiting for transfers between devices: 166 us -> 13.4 us
  blocking collectives: 16.1 us -> 67 us
  starting transfers between devices: 23.8 us -> 12.6 us
  other arithmetic: 36.4 us -> 43.2 us
  matrix products: 7.33 us -> 3.55 us
    psum x1 -> x0, waiting for transfers between devices: 68.6 us -> none  [per_device(): gram_matrix, cross_matrix = lax.psum((gram_part, cross_part), 'tile')]
    unnamed x4 -> x1, waiting for transfers between devices: 62.3 us -> 0.02 us
    all_gather x2 -> x1, blocking collectives: 10.5 us -> 67 us  [per_device(): every = lax.all_gather(well_rates, ('member', 'tile'), axis=0)]
    reduce_scatter x1 -> x0, waiting for transfers between devices: 27.7 us -> none  [per_device(): lax.psum_scatter(lax.dot_general(own_rows, anomaly, contract, preferred_e...]
    ppermute x8 -> x2, starting transfers between devices: 23.5 us -> 6.15 us  [the longest x1 4.86 us: halo_rows(): lax.ppermute(lax.slice_in_dim(block, block.shape[dim] - width, None, axis...]
    all_to_all x0 -> x1, waiting for transfers between devices: none -> 6.59 us  [per_device(): lax.all_to_all(partial_rates.reshape(local_count, tile_count, well_share)...]
    all_to_all x0 -> x1, starting transfers between devices: none -> 6.46 us  [per_device(): lax.all_to_all(partial_rates.reshape(local_count, tile_count, well_share)...]
    psum x1 -> x0, blocking collectives: 5.66 us -> none  [per_device(): mean_rate = lax.psum(jnp.sum(well_rates, 0), 'member') / members]
  transfers between devices with their start and end apart: 11 -> 4, of which waited for: 6 -> 2; matrix products, arithmetic and copies ran while one was open for 4% -> 34% of each run, Pallas kernels for 0% -> 0%
where the time goes in v1:
time: 177 us
  blocking collectives  67 us (38%)
  other arithmetic  43.2 us (24%)
  local copies, waits for them, and re-layouts  21.4 us (12%)
  between operations  15.4 us (9%)
  waiting for transfers between devices  13.4 us (8%)
  starting transfers between devices  12.6 us (7%)
  matrix products  3.55 us (2%)
    all_gather x1, blocking collectives, per_device(): every = lax.all_gather(well_rates, ('member', 'tile'), axis=0)  67 us
    another operation x3, other arithmetic, solve_spd(): jnp.linalg.cholesky(gram_matrix + jnp.eye(gram_matrix.shape[0], dtype=jnp...  12.4 us
    another operation x2, other arithmetic, solve_spd(): lax.linalg.triangular_solve(factor, halfway, left_side=True, lower=True,...  10.4 us
    div x2, other arithmetic, jacobi(): return (baseline + flow_sum) / (storage_term + weight_sum)  6.8 us
    ppermute x1, waiting for transfers between devices, halo_rows(): lax.ppermute(lax.slice_in_dim(block, block.shape[dim] - width, None, axis...  6.76 us
    all_to_all x1, waiting for transfers between devices, per_device(): lax.all_to_all(partial_rates.reshape(local_count, tile_count, well_share)...  6.59 us
    all_to_all x1, starting transfers between devices, per_device(): lax.all_to_all(partial_rates.reshape(local_count, tile_count, well_share)...  6.46 us
    ppermute x1, starting transfers between devices, halo_rows(): lax.ppermute(lax.slice_in_dim(block, block.shape[dim] - width, None, axis...  4.86 us
  transfers between devices with their start and end apart: 4, of which 2 were waited for; matrix products, arithmetic and copies ran while one was open for 34% of the time, Pallas kernels for 0%

profile of v1, /device:TPU:0, one launch (start us, length us, event | category | flops | bytes accessed | tf_op | source)
XLA Modules:
  0.0 176.5 jit_solution(958553342633924820)
XLA Ops:
  7.2 1.9 %copy.82 = bf16[32,4,8,256]{3,0,2,1:T(8,128)(2,1)S(1)} copy(f32[32,4,8,256]{3,2,1,0:T(8,128)} %param.14) | data formatting | bytes 1572864 | tf_op args[0]
  9.1 0.8 bitcast_convert_fusion.3
  9.9 0.8 bitcast_convert_fusion.2
  10.7 0.8 bitcast_convert_fusion.1
  11.5 0.8 bitcast_convert_fusion
  12.3 0.3 concatenate.11
  12.7 4.9 %collective-permute-start = (bf16[36,4,3,256]{3,0,2,1:T(8,128)(2,1)S(1)}, bf16[36,4,3,256]{3,0,2,1:T(8,128)(2,1)S(1)}, u32[]{:S(2)}, u32[]{:S(2)}) collective-permute-start(bf16[36,4,3,256]{3,0,2,1:T(8,128)(2,1)S(1)} %get-tuple-element.13), channel_id=1, source_target_pairs={{0,4},{4,8},{8,12},{12,16},{16,20},{20,24},{24,28},{1,5},{5,9},{9,... | collective-permute-start | bytes 663560 | tf_op jit(solution)/shard_map/ppermute | solution.py:19
  17.6 1.3 collective-permute-start.1
  18.9 0.1 multiply_convert_fusion
  19.0 1.1 copy.70
  20.9 0.2 fusion.21
  21.3 6.8 %collective-permute-done = bf16[36,4,3,256]{3,0,2,1:T(8,128)(2,1)S(1)} collective-permute-done((bf16[36,4,3,256]{3,0,2,1:T(8,128)(2,1)S(1)}, bf16[36,4,3,256]{3,0,2,1:T(8,128)(2,1)S(1)}, u32[]{:S(2)}, u32[]{:S(2)}) %collective-permute-start) | collective-permute-done | bytes 221216 | tf_op jit(solution)/shard_map/ppermute | solution.py:19
  28.0 0.2 copy_convert_fusion.2
  28.2 0.1 slice.215
  28.3 0.2 copy_convert_fusion.1
  28.5 0.1 slice.217
  29.0 0.5 maximum_exponential_fusion
  29.5 0.6 add_divide_fusion
  30.1 0.3 divide_multiply_fusion.1
  30.4 0.6 divide_multiply_fusion
  31.1 0.2 broadcast_in_dim.114
  31.4 0.3 broadcast_in_dim.115
  31.6 0.3 broadcast_in_dim.112
  31.9 0.3 broadcast_in_dim.113
  32.1 0.2 broadcast_in_dim.116
  32.3 0.2 broadcast_in_dim.117
  32.5 3.5 %fusion.3 = f32[32,4,14,256]{3,2,1,0:T(8,128)S(1)} fusion(f32[32,3,14,256]{3,2,1,0:T(8,128)S(1)} %divide_multiply_fusion.1, f32[32,3,14,256]{3,2,1,0:T(8,128)S(1)} %broadcast_in_dim.117, f32[32,3,14,256]{3,2,1,0:T(8,128)S(1)} %broadcast_in_dim.116, f32[32,4,14,255]{3,2,1,0:T(8,128)S(1)} %broadcast_in_dim.115, f32[32,4,14,255]{3,2,1,0:T(8,128)S(1)} %broadcast_in_dim.114, ...), kind=kLoop, calls=%fused_computation.11 | loop fusion | flops 8716288 | bytes 16673792 | tf_op jit(solution)/shard_map/div | solution.py:71
  36.0 0.8 fusion.55
  36.8 0.7 fusion.54
  37.5 0.5 fusion.56
  38.1 3.3 %fusion.7 = f32[32,4,14,256]{3,2,1,0:T(8,128)S(1)} fusion(f32[32,3,14,256]{3,2,1,0:T(8,128)S(1)} %divide_multiply_fusion.1, f32[32,3,14,256]{3,2,1,0:T(8,128)S(1)} %get-tuple-element.12, f32[32,3,14,256]{3,2,1,0:T(8,128)S(1)} %get-tuple-element.11, f32[32,4,14,255]{3,2,1,0:T(8,128)S(1)} %get-tuple-element.10, f32[32,4,14,255]{3,2,1,0:T(8,128)S(1)} %get-tuple-element.9, ...), kind=kLoop, calls=%fused_computation.15 | loop fusion | flops 8716288 | bytes 16673792 | tf_op jit(solution)/shard_map/div | solution.py:71
  41.4 1.1 select_multiply_fusion.1
  42.6 1.2 select_multiply_fusion
  43.7 0.8 select_multiply_fusion.2
  44.6 0.2 slice.258
  44.8 2.2 %fusion.12 = (f32[32,4,8,256]{3,2,1,0:T(8,128)S(1)}, f32[32,4,8,256]{3,2,1,0:T(8,128)}) fusion(f32[32,4,14,256]{3,2,1,0:T(8,128)S(1)} %maximum_exponential_fusion, f32[32,3,14,256]{3,2,1,0:T(8,128)S(1)} %select_multiply_fusion.2, f32[32,4,14,255]{3,2,1,0:T(8,128)S(1)} %select_multiply_fusion, f32[32,4,13,256]{3,2,1,0:T(8,128)S(1)} %select_multiply_fusion.1, ...), kind=kLoop, calls=%fused_computation.36 | loop fusion | flops 3670016 | bytes 8086528 | tf_op jit(solution)/shard_map/mul | solution.py:149
  47.0 2.7 %copy.58 = f32[32,4,8,256]{0,3,2,1:T(8,128)} copy(f32[32,4,8,256]{3,2,1,0:T(8,128)S(1)} %get-tuple-element.5) | data formatting | bytes 2097152 | tf_op jit(solution)/shard_map/mul | solution.py:149
  49.7 2.7 %copy.59 = f32[32,4,8,256]{0,3,2,1:T(8,128)} copy(f32[32,4,8,256]{3,2,1,0:T(8,128)S(1)} %slice.258) | data formatting | bytes 2097152 | tf_op jit(solution)/shard_map/slice | solution.py:103
  52.3 2.9 %gather_fusion = f32[256,32]{1,0:T(8,128)S(1)} fusion(f32[32,8192]{0,1:T(8,128)} %bitcast.97, s32[1024]{0:T(1024)S(1)} %pad_clamp_fusion), kind=kCustom, calls=%fused_computation.clone | custom fusion | bytes 66560 | tf_op jit(solution)/shard_map/jit(_take)/gather | solution.py:151
  55.3 2.9 %gather_fusion.1 = f32[256,32]{1,0:T(8,128)S(1)} fusion(f32[32,8192]{0,1:T(8,128)} %bitcast.96, s32[1024]{0:T(1024)S(1)} %pad_clamp_fusion), kind=kCustom, calls=%fused_computation.1.clone | custom fusion | bytes 66560 | tf_op jit(solution)/shard_map/jit(_take)/gather | solution.py:152
  58.2 0.4 fusion.20
  58.7 0.7 reshape.124
  59.4 6.5 %all-to-all-start = ((f32[8,1,1024]{2,1,0:T(1,128)}), f32[8,1,1024]{2,1,0:T(1,128)S(1)}, u32[]{:S(2)}, u32[]{:S(2)}) async-start(f32[8,1,1024]{2,1,0:T(1,128)} %reshape.124), calls=%async_computation | async-start | bytes 65536 | tf_op jit(solution)/shard_map/all_to_all | solution.py:166
  66.0 6.6 %all-to-all-done = f32[8,1,1024]{2,1,0:T(1,128)S(1)} async-done(((f32[8,1,1024]{2,1,0:T(1,128)}), f32[8,1,1024]{2,1,0:T(1,128)S(1)}, u32[]{:S(2)}, u32[]{:S(2)}) %all-to-all-start) | async-done | bytes 32800 | tf_op jit(solution)/shard_map/all_to_all | solution.py:166
  72.6 0.5 broadcast.213
  73.1 0.7 reduce.7
  73.8 0.1 reshape.125
  73.9 67.0 %all-gather = f32[1024,32]{1,0:T(8,128)S(1)} all-gather(f32[32,32]{1,0:T(8,128)S(1)} %reduce_sum.18), channel_id=2, replica_groups=mesh['tile'=8,'member'=4] {'member','tile'}, dimensions={0}, use_global_device_ids=true | all-gather | bytes 135168 | tf_op jit(solution)/shard_map/all_gather | solution.py:170
  140.9 0.3 copy.83
  141.2 0.3 fusion.52
  141.6 0.3 subtract_divide_fusion
  142.0 0.2 div.81
  142.1 0.3 fusion.60
  142.6 11.7 %cholesky.17 = f32[128,128]{1,0:T(8,128)S(1)} custom-call(f32[128,128]{1,0:T(8,128)S(1)} %fusion.37), custom_call_target="Cholesky" | custom-call | tf_op jit(solution)/shard_map/jit(cholesky)/cholesky | solution.py:95
  154.3 0.6 compare_reduce_fusion
  155.0 0.6 fusion.31
  155.5 9.8 %custom-call.8 = f32[1,128,128]{1,2,0:T(8,128)S(1)} custom-call(f32[1,128,128]{2,1,0:T(8,128)S(1)} %fusion.31), custom_call_target="InvertDiagBlocksLowerTriangular" | custom-call | tf_op jit(solution)/shard_map/triangular_solve | solution.py:97
  165.3 0.2 reshape.95
  165.6 0.3 fusion.30
  165.8 0.2 fusion.34
  166.0 0.2 convolution_convert_fusion
  166.2 2.0 %fusion.61 = f32[32,8192]{1,0:T(8,128)S(1)} fusion(bf16[128,32]{0,1:T(8,128)(2,1)S(1)} %convolution_convert_fusion, bf16[128,8192]{1,0:T(8,128)(2,1)} %all-gather.3.cloned.1.call-done), kind=kOutput, calls=%fused_computation.129 | convolution fusion | flops 67108864 | bytes 3153920 | tf_op jit(solution)/shard_map/dot_general | solution.py:185
  168.2 0.3 copy.71
  168.6 1.1 add.246
  (69 shorter events, 1.4 us)
Async XLA Ops:
  7.2 13.7 %copy-start = (f32[256]{0:T(256)S(1)}, f32[256]{0:T(256)}, u32[]{:S(2)}) copy-start(f32[256]{0:T(256)} %param.19) | copy-start | bytes 3076
  7.2 11.7 %copy-start.2 = (f32[32,4,8,256]{3,2,1,0:T(8,128)S(1)}, f32[32,4,8,256]{3,2,1,0:T(8,128)}, u32[]{:S(2)}) copy-start(f32[32,4,8,256]{3,2,1,0:T(8,128)} %param.14) | copy-start | bytes 3145732
  7.2 159.0 %all-gather.3.cloned.1.call-start = ((), (), s32[]{:S(2)}) async-start(), calls=%async_computation.1 | async-start | bytes 2621440 | tf_op jit(solution)/shard_map/all_gather | solution.py:135
  12.6 7.6 %copy-start.9 = (s32[256]{0:T(256)S(1)}, s32[256]{0:T(256)}, u32[]{:S(2)}) copy-start(s32[256]{0:T(256)} %param.20) | copy-start | bytes 3076
  12.7 8.3 %copy-start.12 = (s32[256]{0:T(256)S(1)}, s32[256]{0:T(256)}, u32[]{:S(2)}) copy-start(s32[256]{0:T(256)} %param.21) | copy-start | bytes 3076
  12.7 15.3 %collective-permute-start = (bf16[36,4,3,256]{3,0,2,1:T(8,128)(2,1)S(1)}, bf16[36,4,3,256]{3,0,2,1:T(8,128)(2,1)S(1)}, u32[]{:S(2)}, u32[]{:S(2)}) collective-permute-start(bf16[36,4,3,256]{3,0,2,1:T(8,128)(2,1)S(1)} %get-tuple-element.13), channel_id=1, source_target_pairs={{0,4},{4,8},{8,12},{12,16},{16,20},{20,24},{24,28},{1,5},{5,9},{9,... | collective-permute-start | bytes 663560 | tf_op jit(solution)/shard_map/ppermute | solution.py:19
  17.6 10.7 %collective-permute-start.1 = (bf16[36,4,3,256]{3,0,2,1:T(8,128)(2,1)S(1)}, bf16[36,4,3,256]{3,0,2,1:T(8,128)(2,1)S(1)}, u32[]{:S(2)}, u32[]{:S(2)}) collective-permute-start(bf16[36,4,3,256]{3,0,2,1:T(8,128)(2,1)S(1)} %get-tuple-element.14), channel_id=1, source_target_pairs={{4,0},{8,4},{12,8},{16,12},{20,16},{24,20},{28,24},{5,1},{9,5},{13... | collective-permute-start | bytes 663560 | tf_op jit(solution)/shard_map/ppermute | solution.py:22
  20.1 8.5 %copy-start.4 = (f32[4,8,256]{2,1,0:T(8,128)S(1)}, f32[4,8,256]{2,1,0:T(8,128)}, u32[]{:S(2)}) copy-start(f32[4,8,256]{2,1,0:T(8,128)} %param.15) | copy-start | bytes 98308
  20.1 8.5 %copy-start.5 = (f32[4,8,256]{2,1,0:T(8,128)S(1)}, f32[4,8,256]{2,1,0:T(8,128)}, u32[]{:S(2)}) copy-start(f32[4,8,256]{2,1,0:T(8,128)} %param.16) | copy-start | bytes 98308
  20.2 8.5 %copy-start.6 = (f32[4,8,256]{2,1,0:T(8,128)S(1)}, f32[4,8,256]{2,1,0:T(8,128)}, u32[]{:S(2)}) copy-start(f32[4,8,256]{2,1,0:T(8,128)} %param.17) | copy-start | bytes 98308
  20.2 8.5 %copy-start.7 = (f32[4,8,256]{2,1,0:T(8,128)S(1)}, f32[4,8,256]{2,1,0:T(8,128)}, u32[]{:S(2)}) copy-start(f32[4,8,256]{2,1,0:T(8,128)} %param.18) | copy-start | bytes 98308
  44.7 5.0 %copy-start.3 = (f32[32,4,8,256]{3,2,1,0:T(8,128)}, f32[32,4,8,256]{3,2,1,0:T(8,128)S(1)}, u32[]{:S(2)}) copy-start(f32[32,4,8,256]{3,2,1,0:T(8,128)S(1)} %slice.258) | copy-start | bytes 3145732
  49.7 16.2 %copy-start.10 = (f32[256]{0:T(256)S(1)}, f32[256]{0:T(256)}, u32[]{:S(2)}) copy-start(f32[256]{0:T(256)} %param.24) | copy-start | bytes 3076
  59.4 13.1 %all-to-all-start = ((f32[8,1,1024]{2,1,0:T(1,128)}), f32[8,1,1024]{2,1,0:T(1,128)S(1)}, u32[]{:S(2)}, u32[]{:S(2)}) async-start(f32[8,1,1024]{2,1,0:T(1,128)} %reshape.124), calls=%async_computation | async-start | bytes 65536 | tf_op jit(solution)/shard_map/all_to_all | solution.py:166
  73.9 68.6 %copy-start.8 = (f32[32,32]{1,0:T(8,128)}, f32[32,32]{1,0:T(8,128)S(1)}, u32[]{:S(2)}) copy-start(f32[32,32]{1,0:T(8,128)S(1)} %reduce_sum.18) | copy-start | bytes 12292
  141.2 24.3 %copy-start.11 = (f32[32,256]{1,0:T(8,128)S(1)}, f32[32,256]{1,0:T(8,128)}, u32[]{:S(2)}) copy-start(f32[32,256]{1,0:T(8,128)} %param.25) | copy-start | bytes 98308
  141.2 24.3 %copy-start.13 = (f32[256]{0:T(256)S(1)}, f32[256]{0:T(256)}, u32[]{:S(2)}) copy-start(f32[256]{0:T(256)} %param.23) | copy-start | bytes 3076
  168.2 1.5 copy-start.1
Sparse Core Ops, SparseCore 0:
  20.3 24.9 all-gather.2
